TPU v7x, 256 devices: a whole 4x4x8 slice. The times are simulated.
256 devices in a mesh: blk: 128 (over y_lo, z, x, core), grp: 2 (over y_hi).
Axes of the slice: x: 4, y: 4 (y_hi: 2, y_lo: 2; y = y_hi * 2 + y_lo), z: 8, core: 2. Of those that a mesh axis runs over, the one named last changes fastest.
Arguments:
- images: bfloat16 [131072, 1024], P(('blk', 'grp')), may hold values from -6 to 6
- texts: bfloat16 [131072, 1024], P(('blk', 'grp')), may hold values from -6 to 6
- row_lse: bfloat16 [131072], P(('blk', 'grp')), may hold values from 6 to 10
- col_lse: bfloat16 [131072], P(('blk', 'grp')), may hold values from 6 to 10
Outputs:
- grad_image: float32 [131072, 1024], P(('blk', 'grp'))
- grad_text: float32 [131072, 1024], P(('blk', 'grp'))
All inputs are finite; a program needn't handle non-finite values.
Results may differ from a plain program's by a relative error of at most 0.0045.
Values may be sent and summed in bfloat16 or wider, within the bound.
A program may use at most 128 MiB of HBM per device.

v0:
```python
import functools
import math

import jax
import jax.numpy as jnp
from jax import lax
from jax.experimental import pallas as pl
from jax.experimental.pallas import tpu as pltpu
from jax.sharding import PartitionSpec as P

MESH = pl.DeviceIdType.MESH
LSE_TOP = 10.0
LOG2E = math.log2(math.e)
PIECES = 4
NX, NZ = 4, 8
ROUTES_2 = (
    (2, 0, 0, 64),
    (2, 1, 64, 64),
    (0, 0, 128, 64),
    (1, 0, 192, 64),
    (1, 1, 256, 64),
    (2, 2, 320, 64),
    (2, 3, 384, 64),
    (0, 7, 448, 64),
)
ROUTES_BACK = (
    (0, 0, 0, 64),
    (1, 6, 64, 64),
    (1, 7, 128, 64),
    (1, 5, 192, 64),
    (3, 0, 256, 64),
    (1, 4, 320, 64),
    (2, 7, 384, 64),
    (2, 0, 448, 64),
)
RELAY_ROWS = 64
Z_SOON, Z_MID = 1, 3


def kernel(
    n_blk,
    scale,
    texts_in,
    images_in,
    row_lse,
    col_lse,
    grad_img,
    grad_txt,
    txt,
    img,
    row_f,
    col_f,
    row_c,
    col_c,
    acc_t,
    acc_i,
    out_t,
    out_1,
    out_2,
    in_t,
    in_1,
    in_2,
    lse_0,
    lse_1,
    load_sem,
    send_sem,
    recv_sem,
    f_send,
    f_recv,
    go_sem,
    ready_sem,
    relay,
    relay_send,
    relay_recv,
):
    rows = texts_in.shape[0]
    half = rows // 2
    part = rows // PIECES
    c = lax.axis_index("blk")
    h = lax.axis_index("grp")
    core = lax.rem(c, 2)
    other = (c, 1 - h)
    sibling = (c + 1 - 2 * core, h)
    ahead = (lax.rem(c + 2, n_blk), h)
    behind = (lax.rem(c + n_blk - 2, n_blk), h)

    x, z, y = lax.rem(c // 2, NX), lax.rem(c // (2 * NX), NZ), c // (2 * NX * NZ)

    def chip(cx, cz, cy):
        return ((cy * NZ + cz) * NX + cx) * 2 + core, h

    def is_at(cx, cz):
        return jnp.logical_and(x == cx, z == cz)

    first, last = is_at(0, 0), is_at(NX - 1, NZ - 1)

    def piece(j, base=0):
        return pl.ds(pl.multiple_of(base + j * part, part), part)

    def remote(src, dst, sends, recvs, to):
        return pltpu.make_async_remote_copy(
            src_ref=src, dst_ref=dst, send_sem=sends, recv_sem=recvs, device_id=to, device_id_type=MESH
        )

    def remote_k(kind, j, src, dst, to):
        return remote(src, dst, send_sem.at[kind, j], recv_sem.at[kind, j], to)

    def send_t(j):
        return remote_k(0, j, texts_in.at[piece(j)], txt.at[piece(j, rows)], other)

    def send_2(j):
        return remote_k(1, j, images_in.at[piece(j)], img.at[2, piece(j)], behind)

    def send_1(j):
        return remote_k(2, j, images_in.at[piece(j)], img.at[1, piece(j)], sibling)

    def pass_1(j):
        return remote_k(2, j, img.at[2, piece(j)], img.at[1, piece(j)], sibling)

    def back_t(j):
        return remote_k(3, j, out_t.at[piece(j)], in_t.at[piece(j)], other)

    def back_1(j):
        return remote_k(4, j, out_1.at[piece(j)], in_1.at[piece(j)], sibling)

    def back_2(j):
        return remote_k(5, j, out_2.at[piece(j)], in_2.at[piece(j)], ahead)

    def send_on(routes, final, src, dst, kind, slot, j):
        for cx, cz, r, n in routes:
            if r // part != j:
                continue
            sem = send_sem.at[kind, j]
            if (cx, cz) == final:
                copy = remote(src.at[pl.ds(r, n)], dst.at[pl.ds(r, n)], sem, recv_sem.at[kind, j], chip(cx, cz, 1 - y))
            else:
                there = relay.at[slot, pl.ds(0, n)]
                copy = remote(src.at[pl.ds(r, n)], there, sem, relay_recv.at[slot], chip(cx, cz, 1 - y))
            copy.start()

    FIRST, LAST = (0, 0), (NX - 1, NZ - 1)

    def send_routes(j, routes=ROUTES_2):
        send_on(routes, LAST, images_in, img.at[2], 1, 0, j)

    def start_2(j):
        @pl.when(jnp.logical_not(first))
        def _():
            send_2(j).start()

        @pl.when(first)
        def _():
            send_routes(j)

    def start_back(j):
        @pl.when(jnp.logical_not(last))
        def _():
            back_2(j).start()

        @pl.when(last)
        def _():
            send_on(ROUTES_BACK, FIRST, out_2, in_2, 5, 1, j)

    def on_route(routes, final, slot, kind, dst, done):
        for cx, cz, r, n in routes:
            if (cx, cz) == final:
                continue

            @pl.when(is_at(cx, cz))
            def _():
                here = relay.at[slot, pl.ds(0, n)]
                if not done:
                    if slot == 0:
                        pl.semaphore_wait(ready_sem.at[1], 1)
                    remote(here, here, relay_send.at[slot], relay_recv.at[slot], chip(*final, y)).wait_recv()
                copy = remote(here, dst.at[pl.ds(r, n)], relay_send.at[slot], recv_sem.at[kind, r // part], chip(*final, y))
                if done:
                    copy.wait_send()
                else:
                    copy.start()

    def pass_2(done=False):
        on_route(ROUTES_2, LAST, 0, 1, img.at[2], done)

    def pass_back(done=False):
        on_route(ROUTES_BACK, FIRST, 1, 5, in_2, done)

    f_t = remote(col_f.at[0], col_f.at[1], f_send.at[0], f_recv.at[0], other)
    f_2 = remote(row_f.at[0], row_f.at[2], f_send.at[1], f_recv.at[1], behind)
    f_1 = remote(row_f.at[0], row_f.at[1], f_send.at[2], f_recv.at[2], sibling)
    f_1_pass = remote(row_f.at[2], row_f.at[1], f_send.at[2], f_recv.at[2], sibling)

    load_t = pltpu.make_async_copy(texts_in, txt.at[pl.ds(0, rows)], load_sem.at[0])
    load_i = pltpu.make_async_copy(images_in, img.at[0], load_sem.at[1])

    lse = (lse_0, lse_1)
    load_l = [
        pltpu.make_async_copy(row_lse, lse_0, load_sem.at[2]),
        pltpu.make_async_copy(col_lse, lse_1, load_sem.at[3]),
    ]
    for copy in load_l:
        copy.start()

    barrier = pltpu.get_barrier_semaphore()

    def greet(device):
        pl.semaphore_signal(barrier, inc=1, device_id=device, device_id_type=MESH)

    def tell(role, device):
        pl.semaphore_signal(ready_sem.at[role], inc=1, device_id=device, device_id_type=MESH)

    between = [(cx, cz) for cx, cz, _, _ in ROUTES_2 if (cx, cz) != LAST]
    soon = [at for at in between if at[1] <= Z_SOON]
    mid = [at for at in between if Z_SOON < at[1] <= Z_MID]
    later = [at for at in between if at[1] > Z_MID]
    back = [(cx, cz) for cx, cz, _, _ in ROUTES_BACK if (cx, cz) != FIRST]

    for device in (other, sibling, behind):
        greet(device)

    @pl.when(jnp.logical_not(last))
    def _():
        greet(ahead)

    greetings = 4 + jnp.where(first, len(soon) - 1, 0) + jnp.where(last, len(between) + len(back), 0)
    for at in between:

        @pl.when(is_at(*at))
        def _():
            greet(chip(*LAST, y))

    for at in soon:

        @pl.when(is_at(*at))
        def _():
            greet(chip(*FIRST, 1 - y))

    for at in mid + later:
        greetings += jnp.where(is_at(*at), 1, 0)

    for at in back:
        greetings += jnp.where(is_at(*at), 1, 0)

        @pl.when(is_at(*at))
        def _():
            greet(chip(*LAST, 1 - y))

    @pl.when(first)
    def _():
        for at in mid + later:
            greet(chip(*at, 1 - y))
        for at in back:
            greet(chip(*at, y))

    load_t.start()
    load_i.start()
    for k, line in enumerate((row_f, col_f)):
        load_l[k].wait()
        factor = jnp.exp(LSE_TOP - lse[k][...].astype(jnp.float32))
        line[0] = jnp.broadcast_to(factor.reshape(1, rows), (8, rows))
    pl.semaphore_wait(barrier, greetings)

    @pl.when(last)
    def _():
        tell(0, chip(*FIRST, 1 - y))
        for at in between:
            tell(1, chip(*at, y))

    for at in mid + later:

        @pl.when(is_at(*at))
        def _():
            tell(2 if at in mid else 0, chip(*FIRST, 1 - y))

    f_t.start()

    @pl.when(jnp.logical_not(first))
    def _():
        f_2.start()


    @pl.when(core == 0)
    def _():
        @pl.when(jnp.logical_not(first))
        def _():
            for j in range(PIECES):
                send_2(j).start()

        @pl.when(first)
        def _():
            for j in range(PIECES):
                send_routes(j, [route for route in ROUTES_2 if route[:2] in soon])

    @pl.when(core == 1)
    def _():
        f_1.start()
        for j in range(PIECES):
            send_t(j).start()
        for j in range(PIECES):
            send_1(j).start()

    acc_t[...] = jnp.zeros(acc_t.shape, jnp.float32)
    acc_i[...] = jnp.zeros(acc_i.shape, jnp.float32)

    def upright(line):
        return jnp.broadcast_to(line, (128, rows)).T

    col_c[pl.ds(0, rows), :] = upright(col_f[0, 0:1, :])

    def weights(s, upright_f, line_f):
        wide = jnp.concatenate([upright_f] * (s.shape[1] // 128), axis=1)
        return jnp.exp2(s * (scale * LOG2E) - LSE_TOP * LOG2E) * (wide + line_f)

    def scores(a, b):
        return lax.dot_general(a, b, (((1,), (1,)), ((), ())), preferred_element_type=jnp.float32)

    def times(a, b):
        return jnp.dot(a, b, preferred_element_type=jnp.float32)

    def turned_times(a, b):
        return lax.dot_general(a, b, (((0,), (0,)), ((), ())), preferred_element_type=jnp.float32)

    def text_half(k, d, diagonal=False):
        at = pl.ds(pl.multiple_of(k * half, half), half)
        t, i = txt[at, :], img[d]
        w = weights(scores(t, i), col_c[at, :], row_f[d, 0:1, :])
        if diagonal:
            t_id = lax.broadcasted_iota(jnp.int32, w.shape, 0) + k * half
            i_id = lax.broadcasted_iota(jnp.int32, w.shape, 1)
            w = w - jnp.where(t_id == i_id, 2.0, 0.0)
        w = w.astype(jnp.bfloat16)
        acc_t[at, :] += times(w, i)
        acc_i[d] += turned_times(w, t)

    def image_half(d, k, g):
        at = pl.ds(pl.multiple_of(k * half, half), half)
        t_at = pl.ds(pl.multiple_of(g * rows, rows), rows)
        t, i = txt[t_at, :], img[d, at, :]
        w = weights(scores(i, t), row_c[d, at, :], col_f[g, 0:1, :]).astype(jnp.bfloat16)
        acc_i[d, at, :] += times(w, t)
        acc_t[t_at, :] += turned_times(w, i)

    def loop(count, body):
        def step(k, carry):
            body(k)
            return carry

        lax.fori_loop(0, count, step, 0)

    load_t.wait()
    load_i.wait()
    loop(2, lambda k: text_half(k, 0, True))

    @pl.when(core == 0)
    def _():
        def take(j):
            send_2(j).wait_recv()
            pass_1(j).start()

        @pl.when(first)
        def _():
            pl.semaphore_wait(ready_sem.at[2], len(mid))
            for j in range(PIECES):
                send_routes(j, [route for route in ROUTES_2 if route[:2] in mid])

        f_1.wait_recv()
        for j in range(PIECES):
            send_1(j).wait_recv()
        loop(2, lambda k: text_half(k, 1))

        @pl.when(first)
        def _():
            pl.semaphore_wait(ready_sem.at[0], len(later) + 1)
            f_2.start()
            for j in range(PIECES):
                send_routes(j, [route for route in ROUTES_2 if route[:2] in later])

        def start_t():
            pl.semaphore_wait(go_sem, 1)
            for j in range(PIECES):
                send_t(j).start()

        pl.when(last)(start_t)
        take(0)
        f_2.wait_recv()
        f_1_pass.start()
        row_c[2] = upright(row_f[2, 0:1, :])

        def both(k):
            @pl.when(k == 0)
            def _():
                take(1)

            @pl.when(k == 1)
            def _():
                pass_2()
                pl.when(jnp.logical_not(last))(start_t)
                take(2)
                take(3)

            image_half(2, k, 0)

        loop(2, both)
        f_t.wait_recv()
        col_c[pl.ds(rows, rows), :] = upright(col_f[1, 0:1, :])
        send_t(0).wait_recv()
        send_t(1).wait_recv()
        loop(3, lambda d: text_half(2, d))
        out_t[pl.ds(0, half), :] = acc_t[pl.ds(rows, half), :].astype(jnp.bfloat16)
        send_t(2).wait_recv()
        send_t(3).wait_recv()
        back_t(0).start()
        back_t(1).start()

        def ending(k):
            text_half(3, 2 - k)

            @pl.when(k == 0)
            def _():
                def on(j):
                    back_1(j).wait_recv()
                    both = acc_i[2, piece(j), :] + in_1[piece(j), :].astype(jnp.float32)
                    out_2[piece(j), :] = both.astype(jnp.bfloat16)
                    start_back(j)

                for j in range(PIECES):
                    on(j)

            @pl.when(k == 1)
            def _():
                out_1[...] = acc_i[1].astype(jnp.bfloat16)
                loop(PIECES, lambda j: back_1(j).start())

        loop(3, ending)
        out_t[pl.ds(half, half), :] = acc_t[pl.ds(rows + half, half), :].astype(jnp.bfloat16)
        back_t(2).start()
        back_t(3).start()

    @pl.when(core == 1)
    def _():
        f_t.wait_recv()
        col_c[pl.ds(rows, rows), :] = upright(col_f[1, 0:1, :])
        send_t(0).wait_recv()
        send_t(1).wait_recv()
        pl.semaphore_signal(go_sem, inc=1, device_id=sibling, device_id_type=MESH)
        text_half(2, 0)
        f_1.wait_recv()
        row_c[1] = upright(row_f[1, 0:1, :])

        def near(k):
            send_1(2 * k).wait_recv()
            send_1(2 * k + 1).wait_recv()

            @pl.when(k == 0)
            def _():
                @pl.when(first)
                def _():
                    pl.semaphore_wait(ready_sem.at[2], len(mid))
                    pl.semaphore_wait(ready_sem.at[0], len(later) + 1)
                    f_2.start()

                for j in range(PIECES):
                    start_2(j)

            image_half(1, k, 0)

        loop(2, near)
        send_t(2).wait_recv()
        send_t(3).wait_recv()

        def beside(k):
            text_half(2 + jnp.minimum(k, 1), 1 - k // 2)

            @pl.when(k == 1)
            def _():
                out_1[...] = acc_i[1].astype(jnp.bfloat16)
                loop(PIECES, lambda j: back_1(j).start())
                pass_2()

        loop(3, beside)
        f_2.wait_recv()
        row_c[2] = upright(row_f[2, 0:1, :])

        def far(k):
            send_2(2 * k).wait_recv()
            send_2(2 * k + 1).wait_recv()

            def side(g):
                image_half(2, k, 1 - g)

                @pl.when(jnp.logical_and(k == 1, g == 0))
                def _():
                    out_t[...] = acc_t[pl.ds(rows, rows), :].astype(jnp.bfloat16)
                    loop(PIECES, lambda j: back_t(j).start())

            loop(2, side)
            at = pl.ds(pl.multiple_of(k * half, half), half)
            out_2[at, :] = acc_i[2, at, :].astype(jnp.bfloat16)
            for j in range(2):

                @pl.when(k == j)
                def _():
                    start_back(2 * j)
                    start_back(2 * j + 1)

        loop(2, far)

        def near_back(j):
            back_1(j).wait_recv()
            acc_i[0, piece(j), :] += in_1[piece(j), :].astype(jnp.float32)

        loop(PIECES, near_back)

    pass_back()

    def finish(j):
        back_t(j).wait_recv()
        grad_txt[piece(j), :] = acc_t[piece(j), :] + in_t[piece(j), :].astype(jnp.float32)
        back_2(j).wait_recv()
        grad_img[piece(j), :] = acc_i[0, piece(j), :] + in_2[piece(j), :].astype(jnp.float32)

    loop(PIECES, finish)

    f_t.wait_send()
    f_2.wait_send()
    f_1.wait_send()

    def sent(j):
        for copy in (send_t, send_2, send_1, back_t, back_1, back_2):
            copy(j).wait_send()

    loop(PIECES, sent)

    pass_2(done=True)
    pass_back(done=True)


def store(grad_img, grad_txt, img_out, txt_out, sem):
    rows = grad_img.shape[0] // PIECES
    copies = []
    for j in range(PIECES):
        for k, (src, dst) in enumerate(((grad_img, img_out), (grad_txt, txt_out))):
            at = pl.ds(j * rows, rows)
            copies.append(pltpu.make_async_copy(src.at[at], dst.at[at], sem.at[k, j]))
    for copy in copies:
        copy.start()
    for copy in copies:
        copy.wait()


def local(n_blk, images, texts, row_lse, col_lse):
    rows, width = images.shape
    scale = 2.0 / math.sqrt(width)
    bf16, f32 = jnp.bfloat16, jnp.float32
    any_spec = pl.BlockSpec(memory_space=pl.ANY)
    hbm_spec = pl.BlockSpec(memory_space=pltpu.HBM)
    vmem_spec = pl.BlockSpec(memory_space=pltpu.VMEM)
    grads = pl.pallas_call(
        functools.partial(kernel, n_blk, scale),
        out_shape=[pltpu.VMEM((rows, width), f32)] * 2,
        in_specs=[hbm_spec] * 4,
        out_specs=[vmem_spec] * 2,
        scratch_shapes=[
            pltpu.VMEM((2 * rows, width), bf16),
            pltpu.VMEM((3, rows, width), bf16),
            pltpu.VMEM((3, 8, rows), f32),
            pltpu.VMEM((2, 8, rows), f32),
            pltpu.VMEM((3, rows, 128), f32),
            pltpu.VMEM((2 * rows, 128), f32),
            pltpu.VMEM((2 * rows, width), f32),
            pltpu.VMEM((3, rows, width), f32),
        ]
        + [pltpu.VMEM((rows, width), bf16)] * 6
        + [
            pltpu.VMEM((rows,), bf16),
            pltpu.VMEM((rows,), bf16),
            pltpu.SemaphoreType.DMA((4,)),
            pltpu.SemaphoreType.DMA((6, PIECES)),
            pltpu.SemaphoreType.DMA((6, PIECES)),
            pltpu.SemaphoreType.DMA((3,)),
            pltpu.SemaphoreType.DMA((3,)),
            pltpu.SemaphoreType.REGULAR,
            pltpu.SemaphoreType.REGULAR((3,)),
            pltpu.VMEM((2, RELAY_ROWS, width), bf16),
            pltpu.SemaphoreType.DMA((2,)),
            pltpu.SemaphoreType.DMA((2,)),
        ],
        compiler_params=pltpu.CompilerParams(
            collective_id=0, has_side_effects=True, vmem_limit_bytes=48 * 2**20
        ),
        cost_estimate=pl.CostEstimate(
            flops=18 * 2 * rows * rows * width,
            bytes_accessed=12 * rows * width,
            transcendentals=6 * rows * rows,
        ),
        name="contrastive",
    )(
        pltpu.with_memory_space_constraint(texts, pltpu.HBM),
        pltpu.with_memory_space_constraint(images, pltpu.HBM),
        pltpu.with_memory_space_constraint(row_lse, pltpu.HBM),
        pltpu.with_memory_space_constraint(col_lse, pltpu.HBM),
    )
    return tuple(
        pl.pallas_call(
            store,
            out_shape=[jax.ShapeDtypeStruct((rows, width), f32)] * 2,
            in_specs=[vmem_spec] * 2,
            out_specs=[any_spec] * 2,
            scratch_shapes=[pltpu.SemaphoreType.DMA((2, PIECES))],
            compiler_params=pltpu.CompilerParams(vmem_limit_bytes=16 * 2**20),
            name="store",
        )(*grads)
    )


def solution(mesh):
    both = ("blk", "grp")
    return jax.shard_map(
        functools.partial(local, mesh.shape["blk"]),
        mesh=mesh,
        in_specs=(P(both, None), P(both, None), P(both), P(both)),
        out_specs=(P(both, None), P(both, None)),
        check_vma=False,
    )
```

profile of v0, /device:TPU:1, one launch (start us, length us, event | category | flops | bytes accessed | tf_op | source)
XLA Modules:
  0.0 62.2 jit_solution(11718093168155053960)
XLA Ops:
  0.6 59.5 %contrastive.1 = (f32[512,1024]{1,0:T(8,128)S(1)}, f32[512,1024]{1,0:T(8,128)S(1)}) custom-call(bf16[512,1024]{1,0:T(8,128)(2,1)} %texts_in.1, bf16[512,1024]{1,0:T(8,128)(2,1)} %images_in.1, bf16[512]{0:T(512)(128)(2,1)} %row_lse.1, bf16[512]{0:T(512)(128)(2,1)} %col_lse.1), custom_call_target="tpu_custom_call" | custom-call | flops 9663676416 | bytes 6291456 | tf_op jit(solution)/shard_map/contrastive/pallas_call | solution.py:558
  60.2 2.1 %store.1 = (f32[512,1024]{1,0:T(8,128)}, f32[512,1024]{1,0:T(8,128)}) custom-call(f32[512,1024]{1,0:T(8,128)S(1)} %get-tuple-element.4.grad_img, f32[512,1024]{1,0:T(8,128)S(1)} %get-tuple-element.5.grad_txt), custom_call_target="tpu_custom_call" | custom-call | tf_op jit(solution)/shard_map/store/pallas_call | solution.py:604
where the time goes:
time: 62.8 us; the launch traced here: 62.2 us
  Pallas kernels  61.6 us (98%)
  between operations  0.64 us (1%)
    pallas_call x1, Pallas kernels, local(): pl.pallas_call(functools.partial(kernel, n_blk, scale), out_shape=[pltpu....  59.5 us
    pallas_call x1, Pallas kernels, local(): pl.pallas_call(store, out_shape=[jax.ShapeDtypeStruct((rows, width), f32)...  2.07 us

commit v1 on v0

--- a/solution.py
+++ b/solution.py
@@ -16,22 +16,22 @@
 ROUTES_2 = (
     (2, 0, 0, 64),
     (2, 1, 64, 64),
-    (0, 0, 128, 64),
-    (1, 0, 192, 64),
-    (1, 1, 256, 64),
-    (2, 2, 320, 64),
-    (2, 3, 384, 64),
-    (0, 7, 448, 64),
+    (1, 0, 128, 64),
+    (1, 1, 192, 64),
+    (2, 2, 256, 64),
+    (2, 3, 320, 64),
+    (0, 7, 384, 64),
+    (2, 4, 448, 64),
 )
 ROUTES_BACK = (
-    (0, 0, 0, 64),
+    (3, 0, 0, 64),
     (1, 6, 64, 64),
     (1, 7, 128, 64),
     (1, 5, 192, 64),
-    (3, 0, 256, 64),
+    (0, 0, 256, 64),
     (1, 4, 320, 64),
-    (2, 7, 384, 64),
-    (2, 0, 448, 64),
+    (2, 0, 384, 64),
+    (1, 3, 448, 64),
 )
 RELAY_ROWS = 64
 Z_SOON, Z_MID = 1, 3
@@ -443,6 +443,12 @@
         send_t(0).wait_recv()
         send_t(1).wait_recv()
         pl.semaphore_signal(go_sem, inc=1, device_id=sibling, device_id_type=MESH)
+
+        @pl.when(last)
+        def _():
+            for j in range(PIECES):
+                send_2(j).start()
+
         text_half(2, 0)
         f_1.wait_recv()
         row_c[1] = upright(row_f[1, 0:1, :])
@@ -459,8 +465,10 @@
                     pl.semaphore_wait(ready_sem.at[0], len(later) + 1)
                     f_2.start()
 
-                for j in range(PIECES):
-                    start_2(j)
+                @pl.when(jnp.logical_not(last))
+                def _():
+                    for j in range(PIECES):
+                        start_2(j)
 
             image_half(1, k, 0)
 

time: 62.8 us -> 61.9 us (0.986)
  Pallas kernels: 61.6 us -> 60.7 us
    pallas_call x1, Pallas kernels: 59.5 us -> 58.7 us  [local(): pl.pallas_call(functools.partial(kernel, n_blk, scale), out_shape=[pltpu....]
where the time goes in v1:
time: 61.9 us; the launch traced here: 61.4 us
  Pallas kernels  60.7 us (98%)
  between operations  0.64 us (1%)
    pallas_call x1, Pallas kernels, local(): pl.pallas_call(functools.partial(kernel, n_blk, scale), out_shape=[pltpu....  58.7 us
    pallas_call x1, Pallas kernels, local(): pl.pallas_call(store, out_shape=[jax.ShapeDtypeStruct((rows, width), f32)...  2.07 us

profile of v1, /device:TPU:1, one launch (start us, length us, event | category | flops | bytes accessed | tf_op | source)
XLA Modules:
  0.0 61.4 jit_solution(15968942365082326523)
XLA Ops:
  0.6 58.7 %contrastive.1 = (f32[512,1024]{1,0:T(8,128)S(1)}, f32[512,1024]{1,0:T(8,128)S(1)}) custom-call(bf16[512,1024]{1,0:T(8,128)(2,1)} %texts_in.1, bf16[512,1024]{1,0:T(8,128)(2,1)} %images_in.1, bf16[512]{0:T(512)(128)(2,1)} %row_lse.1, bf16[512]{0:T(512)(128)(2,1)} %col_lse.1), custom_call_target="tpu_custom_call" | custom-call | flops 9663676416 | bytes 6291456 | tf_op jit(solution)/shard_map/contrastive/pallas_call | solution.py:566
  59.3 2.1 %store.1 = (f32[512,1024]{1,0:T(8,128)}, f32[512,1024]{1,0:T(8,128)}) custom-call(f32[512,1024]{1,0:T(8,128)S(1)} %get-tuple-element.4.grad_img, f32[512,1024]{1,0:T(8,128)S(1)} %get-tuple-element.5.grad_txt), custom_call_target="tpu_custom_call" | custom-call | tf_op jit(solution)/shard_map/store/pallas_call | solution.py:612

commit v2 on v1

--- a/solution.py
+++ b/solution.py
@@ -26,7 +26,8 @@
 ROUTES_BACK = (
     (3, 0, 0, 64),
     (1, 6, 64, 64),
-    (1, 7, 128, 64),
+    (1, 7, 128, 32),
+    (2, 6, 160, 32),
     (1, 5, 192, 64),
     (0, 0, 256, 64),
     (1, 4, 320, 64),
@@ -407,10 +408,10 @@
         send_t(1).wait_recv()
         loop(3, lambda d: text_half(2, d))
         out_t[pl.ds(0, half), :] = acc_t[pl.ds(rows, half), :].astype(jnp.bfloat16)
+        back_t(0).start()
+        back_t(1).start()
         send_t(2).wait_recv()
         send_t(3).wait_recv()
-        back_t(0).start()
-        back_t(1).start()
 
         def ending(k):
             text_half(3, 2 - k)

time: 61.9 us -> 62.8 us (1.015)
  Pallas kernels: 60.7 us -> 61.9 us
    pallas_call x1, Pallas kernels: 58.7 us -> 59.8 us  [local(): pl.pallas_call(functools.partial(kernel, n_blk, scale), out_shape=[pltpu....]
where the time goes in v2:
time: 62.8 us; the launch traced here: 62.7 us
  Pallas kernels  61.9 us (99%)
  between operations  0.8 us (1%)
    pallas_call x1, Pallas kernels, local(): pl.pallas_call(functools.partial(kernel, n_blk, scale), out_shape=[pltpu....  59.8 us
    pallas_call x1, Pallas kernels, local(): pl.pallas_call(store, out_shape=[jax.ShapeDtypeStruct((rows, width), f32)...  2.07 us

profile of v2, /device:TPU:1, one launch (start us, length us, event | category | flops | bytes accessed | tf_op | source)
XLA Modules:
  0.0 62.7 jit_solution(4442733470097272227)
XLA Ops:
  0.6 59.8 %contrastive.1 = (f32[512,1024]{1,0:T(8,128)S(1)}, f32[512,1024]{1,0:T(8,128)S(1)}) custom-call(bf16[512,1024]{1,0:T(8,128)(2,1)} %texts_in.1, bf16[512,1024]{1,0:T(8,128)(2,1)} %images_in.1, bf16[512]{0:T(512)(128)(2,1)} %row_lse.1, bf16[512]{0:T(512)(128)(2,1)} %col_lse.1), custom_call_target="tpu_custom_call" | custom-call | flops 9663676416 | bytes 6291456 | tf_op jit(solution)/shard_map/contrastive/pallas_call | solution.py:567
  60.5 2.1 %store.1 = (f32[512,1024]{1,0:T(8,128)}, f32[512,1024]{1,0:T(8,128)}) custom-call(f32[512,1024]{1,0:T(8,128)S(1)} %get-tuple-element.4.grad_img, f32[512,1024]{1,0:T(8,128)S(1)} %get-tuple-element.5.grad_txt), custom_call_target="tpu_custom_call" | custom-call | tf_op jit(solution)/shard_map/store/pallas_call | solution.py:613
